TPU v7x, 256 devices: a whole 4x4x8 slice. The times are simulated.
256 devices in a mesh: leaf: 64 (over x, z, core), blk: 4 (over y).
Axes of the slice: x: 4, y: 4, z: 8, core: 2. Of those that a mesh axis runs over, the one named last changes fastest.
Arguments:
- features: float32 [64, 262144], P(None, ('leaf', 'blk')), may hold values from -6 to 6
- sketch: float32 [256, 262144], P(None, ('leaf', 'blk')), may hold values from -12 to 12
- omega: float32 [256, 262144], P(None, ('leaf', 'blk')), may hold values from -6 to 6
- slot: int32 [262144], P(('leaf', 'blk')), may hold values from 0 to 262143, as said below
- column_order: int32 [6, 256], replicated, may hold values from 0 to 255, each once within a row
Outputs:
- leaf_basis: float32 [256, 262144], P(None, ('leaf', 'blk'))
- transfers: float32 [64, 6, 512, 256], P('leaf')
Inputs may be any that keep to these rules, and one draw needn't show every extreme that they name: slot is a permutation of all points; a point goes to a device with the same blk index as its own, and every device sends exactly 1024 // 64 of its points to each leaf index.
All inputs are finite; a program needn't handle non-finite values.
Results may differ from a plain program's by a relative error of at most 0.0003.
Values sent between devices are 32-bit elements; how exact they have to be, the bound alone decides.
A program may use at most 128 MiB of HBM per device.

v0:
```python
import functools
import math

import jax
import jax.numpy as jnp
from jax import lax
from jax.experimental import pallas as pl
from jax.experimental.pallas import tpu as pltpu
from jax.sharding import PartitionSpec as P

NN = (((1,), (0,)), ((), ()))
NT = (((1,), (1,)), ((), ()))
TN = (((0,), (0,)), ((), ()))
f32, bf16 = jnp.float32, jnp.bfloat16


def mm(a, b, dims):
    return lax.dot_general(a, b, dims, preferred_element_type=f32)


def halves(x):
    hi = x.astype(bf16)
    return hi, (x - hi.astype(f32)).astype(bf16)


def thirds(x):
    hi = x.astype(bf16)
    rest = x - hi.astype(f32)
    mid = rest.astype(bf16)
    return hi, mid, (rest - mid.astype(f32)).astype(bf16)


def dot3(a, b, dims):
    return mm(a[0], b[0], dims) + (mm(a[0], b[1], dims) + mm(a[1], b[0], dims))


def dotf(a, b, dims):
    return dot3(halves(a), halves(b), dims)


def pick(x, hot, dims, left):
    hi, lo = halves(x)
    if left:
        return mm(hi, hot, dims) + mm(lo, hot, dims)
    return mm(hot, hi, dims) + mm(hot, lo, dims)


NB = 32
TILE = 8


def spread_row(x, i):
    return jnp.broadcast_to(x[i:i + 1, :], x.shape)


def diag_inverses(blocks):
    tiles = NB // TILE
    width = 128 * len(blocks)
    a = [jnp.concatenate([x[TILE * q:TILE * q + TILE] for x in blocks], axis=1) for q in range(tiles)]
    lane = lax.broadcasted_iota(jnp.int32, (TILE, width), 1) % NB
    row = lax.broadcasted_iota(jnp.int32, (TILE, width), 0)
    base = lax.broadcasted_iota(jnp.int32, (TILE, 128), 1) // NB * NB
    b = [jnp.where(lane == row + TILE * q, 1.0, 0.0).astype(f32) for q in range(tiles)]

    def column(x, k):
        return jnp.concatenate(
            [jnp.take_along_axis(x[:, 128 * g:128 * g + 128], base + k, axis=1, mode="promise_in_bounds")
             for g in range(len(blocks))], axis=1)

    done = []
    for p in range(tiles):
        below = range(p, tiles)
        cols = [{q: column(a[q], TILE * p + i) for q in below} for i in range(TILE)]
        mult = []
        scale = jnp.zeros((TILE, width), f32)
        for i in range(TILE):
            root = lax.rsqrt(spread_row(cols[i][p], i))
            scale = jnp.where(row == i, root, scale)
            m = {q: cols[i][q] * (root * root) for q in below}
            m[p] = jnp.where(row > i, m[p], 0.0)
            mult.append(m)
            for t in range(i + 1, TILE):
                head = spread_row(cols[t][p], i)
                for q in below:
                    cols[t][q] = cols[t][q] - m[q] * head
            if i + 1 < TILE:
                a[p] = a[p] - m[p] * spread_row(a[p], i)
                b[p] = b[p] - m[p] * spread_row(b[p], i)
        for i in range(TILE):
            ra, rb = spread_row(a[p], i), spread_row(b[p], i)
            for q in range(p + 1, tiles):
                a[q] = a[q] - mult[i][q] * ra
                b[q] = b[q] - mult[i][q] * rb
        done.append(b[p] * scale)
    whole = jnp.concatenate(done, axis=0)
    return [whole[:, 128 * g:128 * g + 128] for g in range(len(blocks))]


def tri_kernel(n_inv_groups, order_ref, gram_ref, second_ref, rhs_ref, basis_ref, trans_ref,
               own, sib, panel, inv, fact, finv):
    groups = 4
    size = order_ref.shape[1]
    half = size // 2
    steps = size // NB
    depth = order_ref.shape[0]
    slots = 2 * depth + 1
    isub = lax.broadcasted_iota(jnp.int32, (size, size), 0)
    hot = [jnp.where(isub == order_ref[l:l + 1, :], 1.0, 0.0).astype(bf16) for l in range(depth)]
    total = [hot[0]]
    for l in range(1, depth):
        total.append(mm(total[-1], hot[l], NN).astype(bf16))

    def reorder(g, q):
        return pick(pick(g, q, NN, True), q, TN, False)

    def unfold(at):
        low = gram_ref[at, half:2 * half, :]
        top = jnp.concatenate([gram_ref[at, 0:half, :], jnp.transpose(low)], axis=1)
        return jnp.concatenate([top, jnp.concatenate([low, gram_ref[at, 2 * half:, :]], axis=1)], axis=0)

    running = unfold(0)
    own[0] = running
    for l in range(depth):
        g = unfold(l + 1)
        sib[l] = g if l == 0 else reorder(g, total[l - 1])
        running = running + g
        own[l + 1] = reorder(running, total[l])

    def dense(s):
        if s <= depth:
            return own, s
        return sib, min(s - depth - 1, depth - 1)

    for j in range(steps):
        for g in range(groups):
            lo = NB * j
            pieces = []
            for t in range(4):
                ref, at = dense(min(4 * g + t, slots - 1))
                pieces.append(ref[at, lo:lo + NB, :])
            panel[g, j] = jnp.concatenate(pieces, axis=0).T

    lane = lax.broadcasted_iota(jnp.int32, (NB, 128), 1)
    rows = lax.broadcasted_iota(jnp.int32, (NB, 128), 0)
    seg_base = (lane // NB) * NB
    r128 = lax.broadcasted_iota(jnp.int32, (128, 128), 0) // NB
    l128 = lax.broadcasted_iota(jnp.int32, (128, 128), 1) // NB
    same = r128 == l128

    same = jnp.where(same, 1.0, 0.0).astype(bf16)

    def spread(x):
        return [jnp.concatenate([part] * 4, axis=0) * same for part in halves(x)]

    def spread_all(blocks, axis):
        return [jnp.concatenate(parts, axis=axis) for parts in zip(*[spread(x) for x in blocks])]

    for j in range(steps):
        lo = NB * j
        nxt = lo + NB
        inverses = diag_inverses([panel[g, j, lo:nxt, :] for g in range(groups)])
        for g in range(groups):
            li = inverses[g]
            lp = dot3(halves(panel[g, j, lo:, :]), spread(li), NT)
            top = jnp.where(lane - seg_base <= rows, lp[:NB], 0.0)
            if lo:
                panel[g, j, :lo, :] = jnp.zeros((lo, 128), f32)
            panel[g, j, lo:nxt, :] = top
            if nxt < size:
                panel[g, j, nxt:, :] = lp[NB:]
                low = lp[NB:]
                lowh = halves(low)
                for i in range(j + 1, steps, 2):
                    at = NB * (i - j - 1)
                    pair = range(i, min(i + 2, steps))
                    rhs = spread_all([low[NB * (k - j - 1):NB * (k - j)] for k in pair], 0)
                    upd = dot3((lowh[0][at:], lowh[1][at:]), rhs, NT)
                    for n, k in enumerate(pair):
                        panel[g, k, NB * k:, :] -= upd[NB * n:, 128 * n:128 * n + 128]
            if g < n_inv_groups:
                lih = halves(li)
                for c in range(0, j + 1, 2):
                    pair = [k for k in (c, c + 1) if k < j]
                    xs = []
                    if pair:
                        prod = dot3(lih, spread_all([inv[g, k, lo:nxt, :] for k in pair], 1), NN)
                        xs = [prod[:, 128 * n:128 * n + 128] for n in range(len(pair))]
                    if c + len(pair) == j and len(pair) < 2:
                        pair.append(j)
                        xs.append(li)
                    for k, x in zip(pair, xs):
                        inv[g, k, lo:nxt, :] = x
                    if nxt < size:
                        upd = dot3(lowh, spread_all(xs, 1), NN)
                        for n, k in enumerate(pair):
                            piece = upd[:, 128 * n:128 * n + 128]
                            if k == j:
                                inv[g, k, nxt:, :] = -piece
                            else:
                                inv[g, k, nxt:, :] -= piece
                if lo:
                    inv[g, j, :lo, :] = jnp.zeros((lo, 128), f32)

    for j in range(steps):
        for g in range(groups):
            flat = panel[g, j].T
            for t in range(4):
                if 4 * g + t < slots:
                    fact[4 * g + t, NB * j:NB * j + NB, :] = flat[NB * t:NB * t + NB]
            if g < n_inv_groups:
                flat = inv[g, j].T
                for t in range(4):
                    if 4 * g + t <= depth:
                        finv[4 * g + t, NB * j:NB * j + NB, :] = flat[NB * t:NB * t + NB]

    whole = jnp.transpose(finv[0]) * math.sqrt(rhs_ref.shape[0] * lax.axis_size("blk"))
    basis_ref[...] = dotf(whole, rhs_ref[...], NT)
    for l in range(depth):
        v = halves(pick(finv[l + 1] * math.sqrt(2 * size), hot[l], NN, False))
        second = second_ref[l]
        trans_ref[l, pl.ds(pl.multiple_of(second * size, size), size), :] = dot3(halves(fact[l]), v, NN)
        trans_ref[l, pl.ds(pl.multiple_of((1 - second) * size, size), size), :] = dot3(
            halves(fact[depth + 1 + l]), v, NN)


def tri(order, grams, second, rhs):
    depth, size = order.shape
    return pl.pallas_call(
        functools.partial(tri_kernel, 2),
        out_shape=(jax.ShapeDtypeStruct(rhs.shape[::-1], f32), jax.ShapeDtypeStruct((depth, 2 * size, size), f32)),
        in_specs=[pl.BlockSpec(memory_space=pltpu.VMEM), pl.BlockSpec(memory_space=pltpu.VMEM),
                  pl.BlockSpec(memory_space=pltpu.SMEM), pl.BlockSpec(memory_space=pltpu.VMEM)],
        out_specs=[pl.BlockSpec(memory_space=pltpu.VMEM)] * 2,
        scratch_shapes=[
            pltpu.VMEM((depth + 1, size, size), f32),
            pltpu.VMEM((depth, size, size), f32),
            pltpu.VMEM((4, 8, size, 128), f32),
            pltpu.VMEM((2, 8, size, 128), f32),
            pltpu.VMEM((2 * depth + 1, size, size), f32),
            pltpu.VMEM((depth + 1, size, size), f32),
        ],
        compiler_params=pltpu.CompilerParams(vmem_limit_bytes=48 << 20),
    )(order, grams, second, rhs)


MESH = pl.DeviceIdType.MESH


def sum_subtrees(gram, leaf, blk, out_ref, flat, part, run, got, stage, full, sems):
    part_send, part_recv, got_send, got_recv, fwd_send, fwd_recv = sems
    n_blk = lax.axis_size("blk")
    rounds = run.shape[0]
    half = flat.shape[1]
    piece = run.shape[1]

    def mates(r):
        unit = 4 ** r
        digit = (leaf // unit) % 4
        moved = (digit + 1 - 2 * (digit % 2), digit + 2 - 4 * (digit // 2), 3 - digit)
        return [leaf + (m - digit) * unit for m in moved]

    flat[0:half] = gram[0:half, 0:half]
    flat[half:2 * half] = gram[half:, 0:half]
    flat[2 * half:] = gram[half:, half:]
    started = []

    def send(src, dst, s_sem, r_sem, device):
        copy = pltpu.make_async_remote_copy(src_ref=src, dst_ref=dst, send_sem=s_sem, recv_sem=r_sem,
                                            device_id=device, device_id_type=MESH)
        copy.start()
        started.append(copy)
        return copy

    first = []
    for d in range(1, n_blk):
        peer = (blk + d) % n_blk
        first.append(send(flat.at[pl.ds(pl.multiple_of(peer * piece, 8), piece)], part.at[d - 1],
                          part_send.at[d - 1], part_recv.at[d - 1], (leaf, peer)))
    yield
    mine = pl.multiple_of(blk * piece, 8)
    forwards = []

    def forward(slot_at, begin, size):
        for d in range(1, n_blk):
            forwards.append(send(stage.at[pl.ds(begin, size)], full.at[pl.ds(begin, size), pl.ds(mine, piece)],
                                 fwd_send.at[slot_at, d - 1], fwd_recv.at[slot_at, d - 1], (leaf, (blk + d) % n_blk)))

    for copy in first:
        copy.wait_recv()
    run[0] = flat[pl.ds(mine, piece)] + ((part[0] + part[1]) + part[2])
    for r in range(rounds):
        copies = [send(run.at[r], got.at[r, m], got_send.at[r, m], got_recv.at[r, m], (mate, blk))
                  for m, mate in enumerate(mates(r))]
        if r == 0:
            stage[0] = run[0]
            full[0, pl.ds(mine, piece)] = stage[0]
            forward(0, 0, 1)
        else:
            forward(r, 2 * r - 1, 2)
        for copy in copies:
            copy.wait_recv()
        near = got[r, 0]
        far = got[r, 1] + got[r, 2]
        if r + 1 < rounds:
            run[r + 1] = run[r] + near + far
        for k, value in enumerate((near, far)):
            stage[1 + 2 * r + k] = value
            full[1 + 2 * r + k, pl.ds(mine, piece)] = value
    forward(rounds, 2 * rounds - 1, 2)
    for copy in forwards:
        copy.wait_recv()
    for copy in started:
        copy.wait_send()
    out_ref[...] = full[...]


def near_kernel(dims, slot_ref, feat_ref, sketch_ref, omega_ref, sums_ref, rhs_ref,
                hot, back, out_a, out_p, out_s, in_a, in_p, in_s, side, acc, row_aug, gram, off_hi, off_lo,
                flat, part, run, got, stage, full,
                send_sem, recv_sem, side_send, side_recv, *sum_sems):
    count_x, count_z, count_core = dims
    count = count_x * count_z * count_core
    leaf, blk = lax.axis_index("leaf"), lax.axis_index("blk")
    n_blk = lax.axis_size("blk")
    points = slot_ref.shape[1]
    chunk = points // count
    feats = feat_ref.shape[0]
    groups = 4
    per = count // groups
    rank = omega_ref.shape[0]
    lot = out_a.shape[1]
    low = lot - chunk // 2
    wide = points // groups
    strip = min(128, wide)
    in_strip = strip // chunk
    my_core = leaf % count_core
    my_z = (leaf // count_core) % count_z
    my_x = leaf // (count_core * count_z)
    right, left = (blk + 1) % n_blk, (blk + n_blk - 1) % n_blk

    def target(t):
        a = lax.div(t, count_z)
        core = lax.rem(my_core + lax.div(a, count_x) + t, count_core)
        z = lax.rem(my_z + t * 3, count_z)
        x = lax.rem(my_x + a + t, count_x)
        return (x * count_z + z) * count_core + core

    barrier = pltpu.get_barrier_semaphore()

    @pl.loop(1, count)
    def _(t):
        pl.semaphore_signal(barrier, inc=1, device_id=(target(t), blk), device_id_type=MESH)

    for peer in [(blk + d) % n_blk for d in range(1, n_blk)]:
        pl.semaphore_signal(barrier, inc=1, device_id=(leaf, peer), device_id_type=MESH)

    own = slot_ref[...]
    bits = lambda n: n.bit_length() - 1
    goal = own >> bits(points * n_blk)
    dc = ((goal & (count_core - 1)) - my_core) & (count_core - 1)
    dz = (((goal >> bits(count_core)) & (count_z - 1)) - my_z) & (count_z - 1)
    dx = ((goal >> bits(count_core * count_z)) - my_x) & (count_x - 1)
    turn = (dz * 3) & (count_z - 1)
    a = ((dx - turn) & (count_x - 1)) + count_x * ((dc - turn) & (count_core - 1))
    shift = chunk * (turn + count_z * a - goal)
    own_row = own.astype(f32)
    own_col = jnp.transpose(jnp.broadcast_to(own_row, (128, points)))
    at = lax.broadcasted_iota(jnp.int32, (points, 128), 0)
    for c in range(points // 128):
        lanes = slice(128 * c, 128 * c + 128)
        place = jnp.sum(jnp.where(own_col < own_row[:, lanes], 1.0, 0.0), axis=0, keepdims=True).astype(jnp.int32)
        hot[:, lanes] = jnp.where(at == place + shift[:, lanes], 1.0, 0.0).astype(bf16)

    fh, fl = halves(jnp.concatenate([feat_ref[...]] * 2, axis=0))
    ph, pl_low = halves(jnp.broadcast_to((own & (points - 1)).astype(f32), (16, points)))
    first = lax.broadcasted_iota(jnp.int32, (in_strip, chunk // 2, 2 * feats), 2) < feats
    oh, ol = halves(omega_ref[...])

    pairs = ((out_a, in_a), (out_s, in_s), (out_p, in_p))

    def moves(t, which):
        src, dst = pairs[which]
        return pltpu.make_async_remote_copy(
            src_ref=src.at[pl.ds(lax.div(t, in_strip) if which == 2 else t, 1)], dst_ref=dst.at[pl.ds(t, 1)],
            send_sem=send_sem.at[which], recv_sem=recv_sem.at[which, lax.div(t, per)],
            device_id=(target(t), blk), device_id_type=MESH)

    def whole(begin, end, which, g):
        into = pairs[which][1].at[pl.ds(begin, end - begin)]
        return pltpu.make_async_remote_copy(
            src_ref=into, dst_ref=into, send_sem=send_sem.at[which], recv_sem=recv_sem.at[which, g],
            device_id=(target(1), blk), device_id_type=MESH)

    def arrived(g, which):
        return whole(max(1, g * per), (g + 1) * per, which, g)

    for r in range(points // strip):
        h = hot[strip * r:strip * r + strip, :]
        lots = slice(in_strip * r, in_strip * r + in_strip)
        value = mm(h, oh, NT) + mm(h, ol, NT)
        for n in range(rank // 128):
            out_a[lots, chunk * n:chunk * n + chunk, :] = jnp.reshape(
                value[:, 128 * n:128 * n + 128], (in_strip, chunk, 128))
        value = jnp.reshape(mm(h, fh, NT) + mm(h, fl, NT), (in_strip, chunk, 2 * feats))
        out_a[lots, low:, 0:2 * feats] = jnp.where(first, value[:, :chunk // 2], value[:, chunk // 2:])
        out_p[r] = (mm(ph, h, NT) + mm(pl_low, h, NT))[0:1]
        if r == 0:
            pl.semaphore_wait(barrier, count - 1 + n_blk - 1)

        @pl.loop(max(1, in_strip * r), in_strip * r + in_strip)
        def _(t):
            moves(t, 0).start()

    sh, sl = halves(sketch_ref[...])
    for r in range(points // strip):
        h = hot[strip * r:strip * r + strip, :]
        out_s[in_strip * r:in_strip * r + in_strip] = jnp.reshape(
            mm(h, sh, NT) + mm(h, sl, NT), (in_strip, chunk, rank))

        @pl.loop(max(1, in_strip * r), in_strip * r + in_strip)
        def _(t):
            moves(t, 1).start()

    @pl.loop(1, count)
    def _(t):
        moves(t, 2).start()

    in_a[0] = out_a[0]
    in_s[0] = out_s[0]
    in_p[0] = out_p[0]

    def own_side(g, way):
        peer, slot_at = ((right, 0), (left, 1))[way]
        rows = pl.ds(g * per, per)
        return pltpu.make_async_remote_copy(
            src_ref=in_a.at[rows], dst_ref=side.at[slot_at, rows], send_sem=side_send.at[way, g],
            recv_sem=side_recv.at[slot_at, g], device_id=(leaf, peer), device_id_type=MESH)

    def relay(g, way):
        peer = (right, left)[way]
        rows = pl.ds((2 * g + way) * (per // 2), per // 2)
        return pltpu.make_async_remote_copy(
            src_ref=side.at[way, rows], dst_ref=side.at[2, rows], send_sem=side_send.at[2 + way, g],
            recv_sem=side_recv.at[2 + way, g], device_id=(leaf, peer), device_id_type=MESH)

    scale = -2.0 / feats * math.log2(math.e)

    def feats_of(lots):
        cut = lots[:, low:, 0:2 * feats]
        return jnp.reshape(jnp.concatenate([cut[:, :, :feats], cut[:, :, feats:]], axis=1), (wide, feats))

    def omegas_of(lots):
        return jnp.concatenate([jnp.reshape(lots[:, chunk * n:chunk * n + chunk], (wide, 128))
                                for n in range(rank // 128)], axis=1)

    one = jnp.ones((wide, 1), bf16)
    fill = jnp.zeros((wide, 256 - 3 * feats - 6), bf16)

    def arrive(g):
        arrived(g, 0).wait_recv()
        for way in range(2):
            own_side(g, way).start()
        x = feats_of(in_a[g * per:g * per + per])
        norm = thirds(jnp.sum(x * x, axis=1, keepdims=True) * scale)
        xh, xl = halves(x * (-2.0 * scale))
        row_aug[g * wide:g * wide + wide, :] = jnp.concatenate([xh, xh, xl, *norm, one, one, one, fill], axis=1)

    def hand_on(g):
        for way in range(2):
            own_side(g, way).wait_recv()
            relay(g, way).start()

    def absorb(block):
        x = feats_of(block)
        xh, xl = halves(x)
        norm = thirds(jnp.sum(x * x, axis=1, keepdims=True) * scale)
        col_aug = jnp.concatenate([xh, xl, xh, one, one, one, *norm, fill], axis=1)
        om = halves(omegas_of(block))
        for a in range(groups):
            rows = slice(a * wide, a * wide + wide)
            value = jnp.exp2(mm(row_aug[rows, :], col_aug, NT))
            acc[rows, :] += dot3(halves(value), om, NN)

    arrive(0)
    for g in range(1, groups):
        arrive(g)
        hand_on(g - 1)
    acc[...] = jnp.zeros_like(acc)

    @pl.loop(0, groups)
    def _(g):
        absorb(in_a[pl.ds(g * per, per)])

    hand_on(groups - 1)

    @pl.loop(0, 2 * groups)
    def _(i):
        absorb(side[lax.div(i, groups), pl.ds(lax.rem(i, groups) * per, per)])

    @pl.loop(0, groups)
    def _(g):
        for way in range(2):
            relay(g, way).wait_recv()
        absorb(side[2, pl.ds(g * per, per)])

    for g in range(groups):
        arrived(g, 1).wait_recv()
        rows = slice(g * wide, g * wide + wide)
        off = halves(jnp.reshape(in_s[g * per:g * per + per], (wide, rank)) - acc[rows, :])
        off_hi[rows, :], off_lo[rows, :] = off
        term = dot3(off, off, TN)
        if g == 0:
            gram[...] = term
        else:
            gram[...] += term

    steps = sum_subtrees(gram, leaf, blk, sums_ref, flat, part, run, got, stage, full, sum_sems)
    next(steps)
    for g in range(groups):
        arrived(g, 2).wait_recv()
    sub = lax.broadcasted_iota(jnp.int32, (in_strip, 1, strip), 0)
    lane = lax.broadcasted_iota(jnp.int32, (in_strip, 1, strip), 2)
    down = lax.broadcasted_iota(jnp.int32, (points, strip), 0)
    for u in range(points // strip):
        mine = jnp.where(lane // chunk == sub, in_p[u * in_strip:(u + 1) * in_strip], 0.0)
        row = jnp.sum(mine, axis=0).astype(jnp.int32)
        back[:, u * strip:(u + 1) * strip] = jnp.where(down == row, 1.0, 0.0).astype(bf16)
    for r in range(groups):
        rows = slice(r * wide, r * wide + wide)
        rhs_ref[rows, :] = mm(back[rows, :], off_hi[...], NN) + mm(back[rows, :], off_lo[...], NN)
    for _ in steps:
        pass

    for which in range(3):
        whole(1, count, which, 0).wait_send()

    @pl.loop(0, groups)
    def _(g):
        for way in range(2):
            own_side(g, way).wait_send()
            relay(g, way).wait_send()


def near_field(slot, features, sketch, omega, depth):
    feats, points = features.shape
    rank = sketch.shape[0]
    count = lax.axis_size("leaf")
    n_blk = lax.axis_size("blk")
    core = 2
    z = min(8, count // core)
    dims = (count // (core * z), z, core)
    half = rank // 2
    lines = 3 * half
    piece = lines // n_blk
    rounds = depth // 2
    chunk = points // count
    lot = rank // 128 * chunk + chunk // 2
    strip = min(128, points // 4)
    vm = lambda *shape: pltpu.VMEM(shape, f32)
    vb = lambda *shape: pltpu.VMEM(shape, bf16)
    dma = lambda *shape: pltpu.SemaphoreType.DMA(shape)
    return pl.pallas_call(
        functools.partial(near_kernel, dims),
        out_shape=(jax.ShapeDtypeStruct((depth + 1, lines, half), f32), jax.ShapeDtypeStruct((points, rank), f32)),
        in_specs=[pl.BlockSpec(memory_space=pltpu.VMEM)] * 4,
        out_specs=[pl.BlockSpec(memory_space=pltpu.VMEM)] * 2,
        scratch_shapes=[
            vb(points, points), vb(points, points),
            vm(count, lot, 128), vm(points // strip, 1, strip), vm(count, chunk, rank),
            vm(count, lot, 128), vm(count, 1, strip), vm(count, chunk, rank),
            vm(3, count, lot, 128), vm(points, rank), vb(points, 256), vm(rank, rank),
            vb(points, rank), vb(points, rank),
            vm(lines, half), vm(n_blk - 1, piece, half), vm(rounds, piece, half), vm(rounds, 3, piece, half),
            vm(depth + 1, piece, half), vm(depth + 1, lines, half),
            dma(3), dma(3, 4), dma(4, 4), dma(4, 4),
            dma(n_blk - 1), dma(n_blk - 1), dma(rounds, 3), dma(rounds, 3),
            dma(rounds + 1, n_blk - 1), dma(rounds + 1, n_blk - 1),
        ],
        compiler_params=pltpu.CompilerParams(collective_id=0, has_side_effects=True, vmem_limit_bytes=56 << 20),
    )(slot[None], features, sketch, omega)


def per_device(features, sketch, omega, slot, column_order):
    depth = column_order.shape[0]
    sums, turned = near_field(slot, features, sketch, omega, depth)
    second = lax.axis_index("leaf") >> jnp.arange(depth, dtype=jnp.int32) & 1
    leaf_basis, transfers = tri(column_order, sums, second, turned)
    return (leaf_basis, transfers[None])


def solution(mesh):
    placed = (
        P(None, ("leaf", "blk")),
        P(None, ("leaf", "blk")),
        P(None, ("leaf", "blk")),
        P(("leaf", "blk")),
        P(),
    )
    return jax.shard_map(
        per_device,
        mesh=mesh,
        in_specs=placed,
        out_specs=(P(None, ("leaf", "blk")), P("leaf", None, None, None)),
        check_vma=False,
    )
```

profile of v0, /device:TPU:6, one launch (start us, length us, event | category | flops | bytes accessed | tf_op | source)
XLA Modules:
  0.0 140.6 jit_solution(17176229144269432736)
XLA Ops:
  0.6 109.1 %shard_map.68 = (f32[7,384,128]{2,1,0:T(8,128)}, f32[1024,256]{1,0:T(8,128)}) custom-call(s32[1,1024]{1,0:T(1,128)} %bitcast.2, f32[64,1024]{1,0:T(8,128)} %feat_ref.1, f32[256,1024]{1,0:T(8,128)} %sketch_ref.1, f32[256,1024]{1,0:T(8,128)} %omega_ref.1), custom_call_target="tpu_custom_call" | custom-call | tf_op jit(solution)/shard_map/pallas_call | solution.py:562
  109.7 0.0 copy-start
  109.7 1.3 copy-done
  111.1 0.0 copy-start.1
  111.1 1.2 copy-done.1
  112.3 0.0 copy-start.2
  112.3 0.7 copy-done.2
  113.0 27.6 %shard_map.69 = (f32[256,1024]{1,0:T(8,128)}, f32[6,512,256]{2,1,0:T(8,128)}) custom-call(s32[6,256]{1,0:T(8,128)S(1)} %copy-done.2, f32[7,384,128]{2,1,0:T(8,128)S(1)} %copy-done, s32[6]{0:T(128)S(1)} %shift-right-arithmetic_and_fusion.second_ref, f32[1024,256]{1,0:T(8,128)S(1)} %copy-done.1), custom_call_target="tpu_custom_call" | custom-call | tf_op jit(solution)/shard_map/pallas_call | solution.py:228
  (1 shorter events, 0.0 us)
Async XLA Ops:
  109.7 1.3 copy-start
  111.1 1.2 copy-start.1
  112.3 0.7 copy-start.2
where the time goes:
time: 142 us; the launch traced here: 141 us
  Pallas kernels  137 us (96%)
  local copies, waits for them, and re-layouts  3.25 us (2%)
    pallas_call x1, Pallas kernels, near_field(): pl.pallas_call(functools.partial(near_kernel, dims), out_shape=(jax.Shape...  109 us
    pallas_call x1, Pallas kernels, tri(): pl.pallas_call(functools.partial(tri_kernel, 2), out_shape=(jax.ShapeDtyp...  27.6 us
    unnamed x6, local copies, waits for them, and re-layouts  3.25 us

commit v1 on v0

--- a/solution.py
+++ b/solution.py
@@ -97,8 +97,10 @@
 
 
 def tri_kernel(n_inv_groups, order_ref, gram_ref, second_ref, rhs_ref, basis_ref, trans_ref,
-               own, sib, panel, inv, fact, finv):
+               own, sib, panel, inv, fact, finv, rhs_in, basis_out, trans_out, load_sem, store_sem):
     groups = 4
+    load = pltpu.make_async_copy(rhs_ref, rhs_in, load_sem)
+    load.start()
     size = order_ref.shape[1]
     half = size // 2
     steps = size // NB
@@ -137,8 +139,8 @@
             pieces = []
             for t in range(4):
                 ref, at = dense(min(4 * g + t, slots - 1))
-                pieces.append(ref[at, lo:lo + NB, :])
-            panel[g, j] = jnp.concatenate(pieces, axis=0).T
+                pieces.append(ref[at, lo:lo + NB, lo // 128 * 128:])
+            panel[g, j, lo // 128 * 128:, :] = jnp.concatenate(pieces, axis=0).T
 
     lane = lax.broadcasted_iota(jnp.int32, (NB, 128), 1)
     rows = lax.broadcasted_iota(jnp.int32, (NB, 128), 0)
@@ -163,8 +165,8 @@
             li = inverses[g]
             lp = dot3(halves(panel[g, j, lo:, :]), spread(li), NT)
             top = jnp.where(lane - seg_base <= rows, lp[:NB], 0.0)
-            if lo:
-                panel[g, j, :lo, :] = jnp.zeros((lo, 128), f32)
+            if lo % 128:
+                panel[g, j, lo // 128 * 128:lo, :] = jnp.zeros((lo % 128, 128), f32)
             panel[g, j, lo:nxt, :] = top
             if nxt < size:
                 panel[g, j, nxt:, :] = lp[NB:]
@@ -198,29 +200,44 @@
                                 inv[g, k, nxt:, :] = -piece
                             else:
                                 inv[g, k, nxt:, :] -= piece
-                if lo:
-                    inv[g, j, :lo, :] = jnp.zeros((lo, 128), f32)
-
-    for j in range(steps):
-        for g in range(groups):
-            flat = panel[g, j].T
+                if lo % 128:
+                    inv[g, j, lo // 128 * 128:lo, :] = jnp.zeros((lo % 128, 128), f32)
+
+    def unpack(source, into, g, last):
+        for j in range(steps):
+            begin = NB * j // 128 * 128
+            flat = source[g, j, begin:, :].T
             for t in range(4):
-                if 4 * g + t < slots:
-                    fact[4 * g + t, NB * j:NB * j + NB, :] = flat[NB * t:NB * t + NB]
-            if g < n_inv_groups:
-                flat = inv[g, j].T
-                for t in range(4):
-                    if 4 * g + t <= depth:
-                        finv[4 * g + t, NB * j:NB * j + NB, :] = flat[NB * t:NB * t + NB]
-
-    whole = jnp.transpose(finv[0]) * math.sqrt(rhs_ref.shape[0] * lax.axis_size("blk"))
-    basis_ref[...] = dotf(whole, rhs_ref[...], NT)
+                at = 4 * g + t
+                if at < last:
+                    if begin:
+                        into[at, NB * j:NB * j + NB, :begin] = jnp.zeros((NB, begin), f32)
+                    into[at, NB * j:NB * j + NB, begin:] = flat[NB * t:NB * t + NB]
+
+    for g in range(n_inv_groups):
+        unpack(inv, finv, g, depth + 1)
+
+    stores = []
+
+    def store(src, dst):
+        stores.append(pltpu.make_async_copy(src, dst, store_sem.at[len(stores)]))
+        stores[-1].start()
+
+    load.wait()
+    inverse = jnp.transpose(finv[0]) * math.sqrt(rhs_ref.shape[0] * lax.axis_size("blk"))
+    basis_out[...] = dotf(inverse, rhs_in[...], NT)
+    store(basis_out, basis_ref)
+    for g in range(groups):
+        unpack(panel, fact, g, slots)
     for l in range(depth):
         v = halves(pick(finv[l + 1] * math.sqrt(2 * size), hot[l], NN, False))
         second = second_ref[l]
-        trans_ref[l, pl.ds(pl.multiple_of(second * size, size), size), :] = dot3(halves(fact[l]), v, NN)
-        trans_ref[l, pl.ds(pl.multiple_of((1 - second) * size, size), size), :] = dot3(
+        trans_out[l, pl.ds(pl.multiple_of(second * size, size), size), :] = dot3(halves(fact[l]), v, NN)
+        trans_out[l, pl.ds(pl.multiple_of((1 - second) * size, size), size), :] = dot3(
             halves(fact[depth + 1 + l]), v, NN)
+        store(trans_out.at[l], trans_ref.at[l])
+    for copy in stores:
+        copy.wait()
 
 
 def tri(order, grams, second, rhs):
@@ -229,8 +246,8 @@
         functools.partial(tri_kernel, 2),
         out_shape=(jax.ShapeDtypeStruct(rhs.shape[::-1], f32), jax.ShapeDtypeStruct((depth, 2 * size, size), f32)),
         in_specs=[pl.BlockSpec(memory_space=pltpu.VMEM), pl.BlockSpec(memory_space=pltpu.VMEM),
-                  pl.BlockSpec(memory_space=pltpu.SMEM), pl.BlockSpec(memory_space=pltpu.VMEM)],
-        out_specs=[pl.BlockSpec(memory_space=pltpu.VMEM)] * 2,
+                  pl.BlockSpec(memory_space=pltpu.SMEM), pl.BlockSpec(memory_space=pl.ANY)],
+        out_specs=[pl.BlockSpec(memory_space=pl.ANY)] * 2,
         scratch_shapes=[
             pltpu.VMEM((depth + 1, size, size), f32),
             pltpu.VMEM((depth, size, size), f32),
@@ -238,6 +255,11 @@
             pltpu.VMEM((2, 8, size, 128), f32),
             pltpu.VMEM((2 * depth + 1, size, size), f32),
             pltpu.VMEM((depth + 1, size, size), f32),
+            pltpu.VMEM(rhs.shape, f32),
+            pltpu.VMEM(rhs.shape[::-1], f32),
+            pltpu.VMEM((depth, 2 * size, size), f32),
+            pltpu.SemaphoreType.DMA,
+            pltpu.SemaphoreType.DMA((depth + 1,)),
         ],
         compiler_params=pltpu.CompilerParams(vmem_limit_bytes=48 << 20),
     )(order, grams, second, rhs)
@@ -317,7 +339,7 @@
 def near_kernel(dims, slot_ref, feat_ref, sketch_ref, omega_ref, sums_ref, rhs_ref,
                 hot, back, out_a, out_p, out_s, in_a, in_p, in_s, side, acc, row_aug, gram, off_hi, off_lo,
                 flat, part, run, got, stage, full,
-                send_sem, recv_sem, side_send, side_recv, *sum_sems):
+                omega_in, sketch_in, load_sem, send_sem, recv_sem, side_send, side_recv, *sum_sems):
     count_x, count_z, count_core = dims
     count = count_x * count_z * count_core
     leaf, blk = lax.axis_index("leaf"), lax.axis_index("blk")
@@ -345,6 +367,10 @@
         x = lax.rem(my_x + a + t, count_x)
         return (x * count_z + z) * count_core + core
 
+    load_omega = pltpu.make_async_copy(omega_ref, omega_in, load_sem.at[0])
+    load_sketch = pltpu.make_async_copy(sketch_ref, sketch_in, load_sem.at[1])
+    load_omega.start()
+    load_sketch.start()
     barrier = pltpu.get_barrier_semaphore()
 
     @pl.loop(1, count)
@@ -374,7 +400,8 @@
     fh, fl = halves(jnp.concatenate([feat_ref[...]] * 2, axis=0))
     ph, pl_low = halves(jnp.broadcast_to((own & (points - 1)).astype(f32), (16, points)))
     first = lax.broadcasted_iota(jnp.int32, (in_strip, chunk // 2, 2 * feats), 2) < feats
-    oh, ol = halves(omega_ref[...])
+    load_omega.wait()
+    oh, ol = halves(omega_in[...])
 
     pairs = ((out_a, in_a), (out_s, in_s), (out_p, in_p))
 
@@ -411,7 +438,8 @@
         def _(t):
             moves(t, 0).start()
 
-    sh, sl = halves(sketch_ref[...])
+    load_sketch.wait()
+    sh, sl = halves(sketch_in[...])
     for r in range(points // strip):
         h = hot[strip * r:strip * r + strip, :]
         out_s[in_strip * r:in_strip * r + in_strip] = jnp.reshape(
@@ -562,7 +590,7 @@
     return pl.pallas_call(
         functools.partial(near_kernel, dims),
         out_shape=(jax.ShapeDtypeStruct((depth + 1, lines, half), f32), jax.ShapeDtypeStruct((points, rank), f32)),
-        in_specs=[pl.BlockSpec(memory_space=pltpu.VMEM)] * 4,
+        in_specs=[pl.BlockSpec(memory_space=pltpu.VMEM)] * 2 + [pl.BlockSpec(memory_space=pl.ANY)] * 2,
         out_specs=[pl.BlockSpec(memory_space=pltpu.VMEM)] * 2,
         scratch_shapes=[
             vb(points, points), vb(points, points),
@@ -572,7 +600,7 @@
             vb(points, rank), vb(points, rank),
             vm(lines, half), vm(n_blk - 1, piece, half), vm(rounds, piece, half), vm(rounds, 3, piece, half),
             vm(depth + 1, piece, half), vm(depth + 1, lines, half),
-            dma(3), dma(3, 4), dma(4, 4), dma(4, 4),
+            vm(rank, points), vm(rank, points), dma(2), dma(3), dma(3, 4), dma(4, 4), dma(4, 4),
             dma(n_blk - 1), dma(n_blk - 1), dma(rounds, 3), dma(rounds, 3),
             dma(rounds + 1, n_blk - 1), dma(rounds + 1, n_blk - 1),
         ],

time: 142 us -> 141 us (level)
  Pallas kernels: 137 us -> 135 us
where the time goes in v1:
time: 141 us; the launch traced here: 140 us
  Pallas kernels  135 us (96%)
  local copies, waits for them, and re-layouts  3.25 us (2%)
    pallas_call x1, Pallas kernels, near_field(): pl.pallas_call(functools.partial(near_kernel, dims), out_shape=(jax.Shape...  109 us
    pallas_call x1, Pallas kernels, tri(): pl.pallas_call(functools.partial(tri_kernel, 2), out_shape=(jax.ShapeDtyp...  26.8 us
    unnamed x6, local copies, waits for them, and re-layouts  3.25 us

profile of v1, /device:TPU:6, one launch (start us, length us, event | category | flops | bytes accessed | tf_op | source)
XLA Modules:
  0.0 139.5 jit_solution(8604861170223285584)
XLA Ops:
  0.6 108.7 %shard_map.68 = (f32[7,384,128]{2,1,0:T(8,128)}, f32[1024,256]{1,0:T(8,128)}) custom-call(s32[1,1024]{1,0:T(1,128)} %bitcast.2, f32[64,1024]{1,0:T(8,128)} %feat_ref.1, f32[256,1024]{1,0:T(8,128)} %sketch_ref.1, f32[256,1024]{1,0:T(8,128)} %omega_ref.1), custom_call_target="tpu_custom_call" | custom-call | tf_op jit(solution)/shard_map/pallas_call | solution.py:590
  109.3 0.0 copy-start
  109.3 1.3 copy-done
  110.6 0.0 copy-start.1
  110.6 1.2 copy-done.1
  111.9 0.0 copy-start.2
  111.9 0.7 copy-done.2
  112.6 26.8 %shard_map.69 = (f32[256,1024]{1,0:T(8,128)}, f32[6,512,256]{2,1,0:T(8,128)}) custom-call(s32[6,256]{1,0:T(8,128)S(1)} %copy-done.2, f32[7,384,128]{2,1,0:T(8,128)S(1)} %copy-done, s32[6]{0:T(128)S(1)} %shift-right-arithmetic_and_fusion.second_ref, f32[1024,256]{1,0:T(8,128)S(1)} %copy-done.1), custom_call_target="tpu_custom_call" | custom-call | tf_op jit(solution)/shard_map/pallas_call | solution.py:245
  (1 shorter events, 0.0 us)
Async XLA Ops:
  109.3 1.3 copy-start
  110.6 1.2 copy-start.1
  111.9 0.7 copy-start.2

commit v2 on v1

--- a/solution.py
+++ b/solution.py
@@ -604,7 +604,7 @@
             dma(n_blk - 1), dma(n_blk - 1), dma(rounds, 3), dma(rounds, 3),
             dma(rounds + 1, n_blk - 1), dma(rounds + 1, n_blk - 1),
         ],
-        compiler_params=pltpu.CompilerParams(collective_id=0, has_side_effects=True, vmem_limit_bytes=56 << 20),
+        compiler_params=pltpu.CompilerParams(collective_id=0, has_side_effects=True, vmem_limit_bytes=63 << 20),
     )(slot[None], features, sketch, omega)
 
 

time: 141 us -> 141 us (level)
  no operation moved by 1% of the time
where the time goes in v2:
time: 141 us; the launch traced here: 140 us
  Pallas kernels  135 us (96%)
  local copies, waits for them, and re-layouts  3.25 us (2%)
    pallas_call x1, Pallas kernels, near_field(): pl.pallas_call(functools.partial(near_kernel, dims), out_shape=(jax.Shape...  109 us
    pallas_call x1, Pallas kernels, tri(): pl.pallas_call(functools.partial(tri_kernel, 2), out_shape=(jax.ShapeDtyp...  26.8 us
    unnamed x6, local copies, waits for them, and re-layouts  3.25 us

profile of v2, /device:TPU:6, one launch (start us, length us, event | category | flops | bytes accessed | tf_op | source)
XLA Modules:
  0.0 139.5 jit_solution(8024575974321400500)
XLA Ops:
  0.6 108.7 %shard_map.68 = (f32[7,384,128]{2,1,0:T(8,128)}, f32[1024,256]{1,0:T(8,128)}) custom-call(s32[1,1024]{1,0:T(1,128)} %bitcast.2, f32[64,1024]{1,0:T(8,128)} %feat_ref.1, f32[256,1024]{1,0:T(8,128)} %sketch_ref.1, f32[256,1024]{1,0:T(8,128)} %omega_ref.1), custom_call_target="tpu_custom_call" | custom-call | tf_op jit(solution)/shard_map/pallas_call | solution.py:590
  109.3 0.0 copy-start
  109.3 1.3 copy-done
  110.6 0.0 copy-start.1
  110.6 1.2 copy-done.1
  111.9 0.0 copy-start.2
  111.9 0.7 copy-done.2
  112.6 26.8 %shard_map.69 = (f32[256,1024]{1,0:T(8,128)}, f32[6,512,256]{2,1,0:T(8,128)}) custom-call(s32[6,256]{1,0:T(8,128)S(1)} %copy-done.2, f32[7,384,128]{2,1,0:T(8,128)S(1)} %copy-done, s32[6]{0:T(128)S(1)} %shift-right-arithmetic_and_fusion.second_ref, f32[1024,256]{1,0:T(8,128)S(1)} %copy-done.1), custom_call_target="tpu_custom_call" | custom-call | tf_op jit(solution)/shard_map/pallas_call | solution.py:245
  (1 shorter events, 0.0 us)
Async XLA Ops:
  109.3 1.3 copy-start
  110.6 1.2 copy-start.1
  111.9 0.7 copy-start.2

commit v3 on v1

--- a/solution.py
+++ b/solution.py
@@ -97,17 +97,22 @@
 
 
 def tri_kernel(n_inv_groups, order_ref, gram_ref, second_ref, rhs_ref, basis_ref, trans_ref,
-               own, sib, panel, inv, fact, finv, rhs_in, basis_out, trans_out, load_sem, store_sem):
+               own, sib, panel, inv, fact, finv, rhs_in, basis_out, trans_out, order_in, gram_in, load_sem, store_sem):
     groups = 4
-    load = pltpu.make_async_copy(rhs_ref, rhs_in, load_sem)
-    load.start()
     size = order_ref.shape[1]
     half = size // 2
     steps = size // NB
     depth = order_ref.shape[0]
+    load_order = pltpu.make_async_copy(order_ref, order_in, load_sem.at[0])
+    load_grams = pltpu.make_async_copy(gram_ref, gram_in, load_sem.at[2])
+    load = pltpu.make_async_copy(rhs_ref, rhs_in, load_sem.at[1])
+    for copy in (load_order, load_grams, load):
+        copy.start()
+    load_order.wait()
+    load_grams.wait()
     slots = 2 * depth + 1
     isub = lax.broadcasted_iota(jnp.int32, (size, size), 0)
-    hot = [jnp.where(isub == order_ref[l:l + 1, :], 1.0, 0.0).astype(bf16) for l in range(depth)]
+    hot = [jnp.where(isub == order_in[l:l + 1, :], 1.0, 0.0).astype(bf16) for l in range(depth)]
     total = [hot[0]]
     for l in range(1, depth):
         total.append(mm(total[-1], hot[l], NN).astype(bf16))
@@ -116,9 +121,9 @@
         return pick(pick(g, q, NN, True), q, TN, False)
 
     def unfold(at):
-        low = gram_ref[at, half:2 * half, :]
-        top = jnp.concatenate([gram_ref[at, 0:half, :], jnp.transpose(low)], axis=1)
-        return jnp.concatenate([top, jnp.concatenate([low, gram_ref[at, 2 * half:, :]], axis=1)], axis=0)
+        low = gram_in[at, half:2 * half, :]
+        top = jnp.concatenate([gram_in[at, 0:half, :], jnp.transpose(low)], axis=1)
+        return jnp.concatenate([top, jnp.concatenate([low, gram_in[at, 2 * half:, :]], axis=1)], axis=0)
 
     running = unfold(0)
     own[0] = running
@@ -245,8 +250,8 @@
     return pl.pallas_call(
         functools.partial(tri_kernel, 2),
         out_shape=(jax.ShapeDtypeStruct(rhs.shape[::-1], f32), jax.ShapeDtypeStruct((depth, 2 * size, size), f32)),
-        in_specs=[pl.BlockSpec(memory_space=pltpu.VMEM), pl.BlockSpec(memory_space=pltpu.VMEM),
-                  pl.BlockSpec(memory_space=pltpu.SMEM), pl.BlockSpec(memory_space=pl.ANY)],
+        in_specs=[pl.BlockSpec(memory_space=pltpu.HBM), pl.BlockSpec(memory_space=pltpu.HBM),
+                  pl.BlockSpec(memory_space=pltpu.SMEM), pl.BlockSpec(memory_space=pltpu.HBM)],
         out_specs=[pl.BlockSpec(memory_space=pl.ANY)] * 2,
         scratch_shapes=[
             pltpu.VMEM((depth + 1, size, size), f32),
@@ -258,7 +263,9 @@
             pltpu.VMEM(rhs.shape, f32),
             pltpu.VMEM(rhs.shape[::-1], f32),
             pltpu.VMEM((depth, 2 * size, size), f32),
-            pltpu.SemaphoreType.DMA,
+            pltpu.VMEM(order.shape, jnp.int32),
+            pltpu.VMEM(grams.shape, f32),
+            pltpu.SemaphoreType.DMA((3,)),
             pltpu.SemaphoreType.DMA((depth + 1,)),
         ],
         compiler_params=pltpu.CompilerParams(vmem_limit_bytes=48 << 20),

time: 141 us -> 141 us (level)
  no operation moved by 1% of the time
where the time goes in v3:
time: 141 us; the launch traced here: 140 us
  Pallas kernels  136 us (96%)
  local copies, waits for them, and re-layouts  3.25 us (2%)
    pallas_call x1, Pallas kernels, near_field(): pl.pallas_call(functools.partial(near_kernel, dims), out_shape=(jax.Shape...  109 us
    pallas_call x1, Pallas kernels, tri(): pl.pallas_call(functools.partial(tri_kernel, 2), out_shape=(jax.ShapeDtyp...  27 us
    unnamed x6, local copies, waits for them, and re-layouts  3.25 us

profile of v3, /device:TPU:6, one launch (start us, length us, event | category | flops | bytes accessed | tf_op | source)
XLA Modules:
  0.0 139.7 jit_solution(11022476087838297959)
XLA Ops:
  0.6 108.7 %shard_map.68 = (f32[7,384,128]{2,1,0:T(8,128)}, f32[1024,256]{1,0:T(8,128)}) custom-call(s32[1,1024]{1,0:T(1,128)} %bitcast.2, f32[64,1024]{1,0:T(8,128)} %feat_ref.1, f32[256,1024]{1,0:T(8,128)} %sketch_ref.1, f32[256,1024]{1,0:T(8,128)} %omega_ref.1), custom_call_target="tpu_custom_call" | custom-call | tf_op jit(solution)/shard_map/pallas_call | solution.py:597
  109.3 0.0 copy-start
  109.3 1.3 copy-done
  110.6 0.0 copy-start.1
  110.6 1.2 copy-done.1
  111.9 0.0 copy-start.2
  111.9 0.7 copy-done.2
  112.6 27.0 %shard_map.69 = (f32[256,1024]{1,0:T(8,128)}, f32[6,512,256]{2,1,0:T(8,128)}) custom-call(s32[6,256]{1,0:T(8,128)S(1)} %copy-done.2, f32[7,384,128]{2,1,0:T(8,128)S(1)} %copy-done, s32[6]{0:T(128)S(1)} %shift-right-arithmetic_and_fusion.second_ref, f32[1024,256]{1,0:T(8,128)S(1)} %copy-done.1), custom_call_target="tpu_custom_call" | custom-call | tf_op jit(solution)/shard_map/pallas_call | solution.py:250
  (1 shorter events, 0.0 us)
Async XLA Ops:
  109.3 1.3 copy-start
  110.6 1.2 copy-start.1
  111.9 0.7 copy-start.2
